TPU v7x, 128 devices: a whole 4x4x4 slice. The times are simulated.
128 devices in a mesh: seq: 16 (over y, z_lo, core), tp: 4 (over x), rep: 2 (over z_hi).
Axes of the slice: x: 4, y: 4, z: 4 (z_hi: 2, z_lo: 2; z = z_hi * 2 + z_lo), core: 2. Of those that a mesh axis runs over, the one named last changes fastest.
Arguments:
- tokens: bfloat16 [2, 12288, 3072], P('rep', 'seq'), may hold values from -6 to 6
- in_panels: bfloat16 [3072, 4, 4096], P(('seq', 'rep'), None, 'tp'), may hold values from -0.109375 to 0.109375
- out_panel: bfloat16 [4096, 3072], P('tp', ('seq', 'rep')), may hold values from -0.09375 to 0.09375
- decay_power: int32 [32], P('tp'), may hold values from 0 to 8
- boundary: int32 [2], P('rep'), may hold values from 1 to 12287
Outputs:
- layer_out: bfloat16 [2, 12288, 3072], P('rep', 'seq', 'tp')
All inputs are finite; a program needn't handle non-finite values.
Results may differ from a plain program's by a relative error of at most 0.019.
Values may be sent and summed in bfloat16 or wider, within the bound.
A program may use at most 128 MiB of HBM per device.

v0:
```python
import jax
import jax.numpy as jnp
from jax import lax
from jax.sharding import PartitionSpec as P

D = 3072
HDIM = 128
log_half = -0.6931471805599453
epsilon = 1e-06


def attend_block(queries, key_rows, val_rows, log_rate, anchor, prompt_start):
    extent = queries.shape[0]
    positions = anchor + jnp.arange(extent, dtype=jnp.int32)
    newer_mask = positions >= prompt_start
    offsets = (positions[:, None] - positions[None, :]).astype(jnp.float32)
    allowed = (offsets >= 0.0) & (newer_mask[:, None] == newer_mask[None, :])
    weights = jnp.where(
        allowed[None], jnp.exp(log_rate[:, None, None] * jnp.maximum(offsets, 0.0)[None]), 0.0
    )
    scores = jnp.einsum("ihd,jhd->hij", queries, key_rows, preferred_element_type=jnp.float32)
    scores = (scores * weights).astype(jnp.bfloat16)
    within = jnp.einsum("hij,jhd->ihd", scores, val_rows, preferred_element_type=jnp.float32)
    final_pos = anchor + extent - 1
    kept_rows = (newer_mask == (final_pos >= prompt_start)).astype(jnp.float32)
    steps_out = (final_pos - positions).astype(jnp.float32)
    key_scale = jnp.exp(log_rate[None, :] * steps_out[:, None]) * kept_rows[:, None]
    decayed = (key_rows.astype(jnp.float32) * key_scale[:, :, None]).astype(jnp.bfloat16)
    local_state = jnp.einsum("jhd,jhe->hde", decayed, val_rows, preferred_element_type=jnp.float32)
    return (within, local_state)


def local(tokens, in_panels, out_panel, decay_power, boundary):
    slab_rows = tokens[0]
    extent = slab_rows.shape[0]
    seq_count = lax.axis_size("seq")
    own_index = lax.axis_index("seq")
    anchor = own_index * extent
    prompt_start = boundary[0]
    log_rate = log_half * jnp.exp2(decay_power.astype(jnp.float32)) / (extent * seq_count)
    head_count = decay_power.shape[0]
    width = in_panels.shape[2]
    flat_in = lax.optimization_barrier(in_panels.reshape(in_panels.shape[0], 4 * width))
    full_in = lax.all_gather(flat_in, ("seq", "rep"), axis=0, tiled=True)
    full_out = lax.all_gather(out_panel.T, ("seq", "rep"), axis=0, tiled=True)
    projected = jnp.dot(slab_rows, full_in, preferred_element_type=jnp.float32)
    projected = lax.optimization_barrier(projected)
    projected = projected.reshape(extent, 4, head_count, HDIM)
    queries = (jax.nn.silu(projected[:, 0]) * HDIM ** (-0.5)).astype(jnp.bfloat16)
    key_rows = jax.nn.silu(projected[:, 1]).astype(jnp.bfloat16)
    val_rows = projected[:, 2].astype(jnp.bfloat16)
    gate_rows = jax.nn.sigmoid(projected[:, 3])
    within, local_state = attend_block(queries, key_rows, val_rows, log_rate, anchor, prompt_start)
    states = lax.all_gather(local_state.astype(jnp.bfloat16), "seq")
    owners = jnp.arange(seq_count, dtype=jnp.int32)
    between = (own_index - 1 - owners).astype(jnp.float32)
    crossing = prompt_start // extent
    reaches = (owners < own_index) & ~((owners < crossing) & (crossing < own_index))
    carry = jnp.where(
        reaches[:, None],
        jnp.exp(log_rate[None, :] * extent * jnp.maximum(between, 0.0)[:, None]),
        0.0,
    )
    prior_state = jnp.sum(carry[:, :, None, None] * states.astype(jnp.float32), axis=0)
    attended = within
    positions = anchor + jnp.arange(extent, dtype=jnp.int32)
    use_prior = ((positions < prompt_start) | (anchor > prompt_start)).astype(jnp.float32)
    steps_in = jnp.arange(1, extent + 1, dtype=jnp.int32).astype(jnp.float32)
    query_scale = jnp.exp(log_rate[None, :] * steps_in[:, None]) * use_prior[:, None]
    scaled = queries.astype(jnp.float32) * query_scale[:, :, None]
    attended = attended + jnp.einsum(
        "ihd,hde->ihe", scaled, prior_state, precision=lax.Precision.HIGHEST
    )
    square = jnp.mean(attended * attended, axis=-1, keepdims=True)
    gated_rows = (
        (attended * lax.rsqrt(square + epsilon) * gate_rows)
        .astype(jnp.bfloat16)
        .reshape(extent, head_count * HDIM)
    )
    head_partial = lax.dot_general(
        gated_rows, full_out, (((1,), (1,)), ((), ())), preferred_element_type=jnp.float32
    )
    summed = lax.psum_scatter(
        head_partial.astype(jnp.bfloat16), "tp", scatter_dimension=1, tiled=True
    )
    return summed[None]


def solution(mesh):
    return jax.shard_map(
        local,
        mesh=mesh,
        in_specs=(
            P("rep", "seq", None),
            P(("seq", "rep"), None, "tp"),
            P("tp", ("seq", "rep")),
            P("tp"),
            P("rep"),
        ),
        out_specs=P("rep", "seq", "tp"),
        check_vma=False,
    )
```

profile of v0, /device:TPU:1, one launch (start us, length us, event | category | flops | bytes accessed | tf_op | source)
XLA Modules:
  0.0 410.5 jit_solution(10307200429481321164)
XLA Ops:
  6.5 2.3 copy.26
  8.8 0.0 all-gather.9.cloned.1.call-start
  9.6 0.7 broadcast_multiply_fusion
  10.3 0.1 exponential_multiply_fusion
  10.4 145.5 %all-gather.5.cloned.1.call-done = bf16[3072,4096]{1,0:T(8,128)(2,1)} async-done(((bf16[96,4096]{1,0:T(8,128)(2,1)}), bf16[3072,4096]{1,0:T(8,128)(2,1)}) %all-gather.5.cloned.1.call-update) | async-done | bytes 25165840 | tf_op jit(solution)/shard_map/all_gather | solution.py:44
  155.9 26.0 %fusion.5 = f32[768,4096]{1,0:T(8,128)} fusion(bf16[3072,4096]{1,0:T(8,128)(2,1)} %all-gather.5.cloned.1.call-done, bf16[1,768,3072]{2,1,0:T(8,128)(2,1)} %param.5), kind=kOutput, calls=%fused_computation.7 | convolution fusion | flops 19327352832 | bytes 42467328 | tf_op jit(solution)/shard_map/dot_general | solution.py:46
  181.9 12.0 %copy.27 = f32[96,8,32,128]{3,2,1,0:T(8,128)} copy(f32[96,8,32,128]{3,1,2,0:T(8,128)} %bitcast.65) | data formatting | bytes 25165824
  193.9 7.0 %fusion.31 = (f32[768,1,8,128]{3,2,1,0:T(8,128)S(1)}, f32[768,1,8,128]{3,2,1,0:T(8,128)}, f32[768,1,8,128]{3,2,1,0:T(8,128)}) fusion(f32[768,4,8,128]{3,2,1,0:T(8,128)} %bitcast.63), kind=kLoop, calls=%fused_computation.52 | loop fusion | bytes 18874368 | tf_op jit(solution)/shard_map/slice | solution.py:52
  200.9 3.2 slice.17
  204.1 2.9 copy.24
  207.0 4.9 %fusion.21 = bf16[8,128,128]{2,1,0:T(8,128)(2,1)} fusion(f32[768,8]{0,1:T(8,128)S(1)} %get-tuple-element.9, bf16[768,1,8,128]{0,3,2,1:T(8,128)(2,1)} %copy.24, f32[768,1,8,128]{3,2,1,0:T(8,128)} %get-tuple-element.7), kind=kOutput, calls=%fused_computation.31 | convolution fusion | flops 207749120 | bytes 5005312 | tf_op jit(solution)/shard_map/jhd,jhe->hde/dot_general | solution.py:29
  212.0 0.7 all-gather.7.cloned.1.call-update
  212.8 0.1 exponential_select_fusion
  212.9 1.5 fusion.12
  214.4 1.8 convert_maximum_fusion
  216.1 2.5 copy.25
  218.6 13.7 %fusion = f32[8,128,768]{2,1,0:T(8,128)} fusion(f32[768,768]{1,0:T(8,128)} %convert_maximum_fusion, f32[8]{0:T(128)S(1)} %get-tuple-element.11, pred[768,768]{1,0:T(8,128)(4,1)} %fusion.12, bf16[768,1,8,128]{0,3,2,1:T(8,128)(2,1)} %copy.24, f32[768,1,8,128]{3,2,1,0:T(8,128)} %get-tuple-element.7, f32[768,1,8,128]{3,2,1,0:T(8,128)} %get-tuple-element.6), kind=kOutput, calls=%fused_computation.1 | convolution fusion | flops 2443444224 | bytes 13959200 | tf_op jit(solution)/shard_map/hij,jhd->ihd/dot_general | solution.py:23
  232.3 18.1 %all-gather.9.cloned.1.call-done = bf16[128,128,128]{2,1,0:T(8,128)(2,1)} async-done(((bf16[8,128,128]{2,1,0:T(8,128)(2,1)}), bf16[128,128,128]{2,1,0:T(8,128)(2,1)}) %all-gather.9.cloned.1.call-update) | async-done | bytes 4194320 | tf_op jit(solution)/shard_map/all_gather | solution.py:54
  250.4 3.1 fusion.2
  253.5 8.0 %fusion.8 = (f32[768,8]{0,1:T(8,128)S(1)}, f32[8,128,768]{2,1,0:T(8,128)S(1)}) fusion(f32[8,128,768]{2,1,0:T(8,128)} %fusion, f32[8,128,128]{2,1,0:T(8,128)S(1)} %fusion.2, f32[768,8]{0,1:T(8,128)S(1)} %get-tuple-element.8, f32[768,1,8,128]{3,2,1,0:T(8,128)S(1)} %copy-done.1), kind=kOutput, calls=%fused_computation.15 | convolution fusion | flops 1216604160 | bytes 10010624 | tf_op jit(solution)/shard_map/ihd,hde->ihe/dot_general | solution.py:71
  261.5 0.9 fusion.7
  262.4 79.6 %all-gather.7.cloned.1.call-done = bf16[3072,1024]{1,0:T(8,128)(2,1)} async-done(((bf16[96,1024]{1,0:T(8,128)(2,1)}), bf16[3072,1024]{1,0:T(8,128)(2,1)}) %all-gather.7.cloned.1.call-update) | async-done | bytes 6291472 | tf_op jit(solution)/shard_map/all_gather | solution.py:45
  342.0 9.7 %convolution_convert_fusion = bf16[768,3072]{1,0:T(8,128)(2,1)} fusion(bf16[768,1024]{0,1:T(8,128)(2,1)S(1)} %bitcast.68, bf16[3072,1024]{1,0:T(8,128)(2,1)} %all-gather.7.cloned.1.call-done), kind=kOutput, calls=%fused_computation.6 | convolution fusion | flops 4834197504 | bytes 12582912 | tf_op jit(solution)/shard_map/dot_general | solution.py:80
  351.7 52.3 %reduce-scatter.2.cloned.1.call-done = bf16[768,768]{1,0:T(8,128)(2,1)} async-done(((bf16[768,3072]{1,0:T(8,128)(2,1)}), bf16[768,768]{1,0:T(8,128)(2,1)}) %reduce-scatter.2.cloned.1.call-update) | async-done | bytes 1179664 | tf_op jit(solution)/shard_map/reduce_scatter | solution.py:83
  (17 shorter events, 0.2 us)
Async XLA Ops:
  6.5 149.4 %all-gather.5.cloned.1.call-start = ((), (), s32[]{:S(2)}) async-start(), calls=%async_computation.1 | async-start | bytes 25952256 | tf_op jit(solution)/shard_map/all_gather | solution.py:44
  8.8 241.5 %all-gather.9.cloned.1.call-start = ((), (), s32[]{:S(2)}) async-start(), calls=%async_computation.4 | async-start | bytes 4456448 | tf_op jit(solution)/shard_map/all_gather | solution.py:54
  212.0 130.0 %all-gather.7.cloned.1.call-start = ((), (), s32[]{:S(2)}) async-start(), calls=%async_computation.2 | async-start | bytes 6488064 | tf_op jit(solution)/shard_map/all_gather | solution.py:45
  212.7 191.3 %reduce-scatter.2.cloned.1.call-start = ((), (), s32[]{:S(2)}) async-start(), calls=%async_computation.3 | async-start | bytes 5898240 | tf_op jit(solution)/shard_map/reduce_scatter | solution.py:83
  232.3 21.2 %copy-start.1 = (f32[768,1,8,128]{3,2,1,0:T(8,128)S(1)}, f32[768,1,8,128]{3,2,1,0:T(8,128)}, u32[]{:S(2)}) copy-start(f32[768,1,8,128]{3,2,1,0:T(8,128)} %get-tuple-element.6) | copy-start | bytes 9437188
  253.5 8.0 %copy-start = (f32[768,1,8,128]{0,3,2,1:T(8,128)S(1)}, f32[768,1,8,128]{0,3,2,1:T(8,128)}, u32[]{:S(2)}) copy-start(f32[768,1,8,128]{0,3,2,1:T(8,128)} %copy.25) | copy-start | bytes 9437188
Sparse Core Ops, SparseCore 0:
  9.0 146.8 all-gather.4
  212.1 38.2 all-gather.8
  252.1 89.8 all-gather.6
  351.8 52.0 reduce-scatter.1
where the time goes:
time: 411 us; the launch traced here: 410 us
  waiting for transfers between devices  296 us (72%)
  matrix products  62.3 us (15%)
  local copies, waits for them, and re-layouts  29.8 us (7%)
  between operations  13.9 us (3%)
  other arithmetic  8.14 us (2%)
    all_gather x1, waiting for transfers between devices, local(): full_in = lax.all_gather(flat_in, ('seq', 'rep'), axis=0, tiled=True)  146 us
    all_gather x1, waiting for transfers between devices, local(): full_out = lax.all_gather(out_panel.T, ('seq', 'rep'), axis=0, tiled=True)  79.6 us
    reduce_scatter x1, waiting for transfers between devices, local(): lax.psum_scatter(head_partial.astype(jnp.bfloat16), 'tp', scatter_dimensi...  52.3 us
    dot_general x1, matrix products, local(): projected = jnp.dot(slab_rows, full_in, preferred_element_type=jnp.float32)  26 us
    unnamed x8, local copies, waits for them, and re-layouts  19.6 us
    all_gather x1, waiting for transfers between devices, local(): states = lax.all_gather(local_state.astype(jnp.bfloat16), 'seq')  18.1 us
    dot_general x1, matrix products, attend_block(): jnp.einsum('hij,jhd->ihd', scores, val_rows, preferred_element_type=jnp.f...  13.7 us
    dot_general x1, matrix products, local(): lax.dot_general(gated_rows, full_out, (((1,), (1,)), ((), ())), preferred...  9.71 us
  transfers between devices with their start and end apart: 4, of which 4 were waited for; matrix products, arithmetic and copies ran while one was open for 8% of the time, Pallas kernels for 0%

commit v1 on v0

--- a/solution.py
+++ b/solution.py
@@ -41,7 +41,10 @@
     head_count = decay_power.shape[0]
     width = in_panels.shape[2]
     flat_in = lax.optimization_barrier(in_panels.reshape(in_panels.shape[0], 4 * width))
-    full_in = lax.all_gather(flat_in, ("seq", "rep"), axis=0, tiled=True)
+    full_in = jnp.concatenate(
+        lax.all_to_all(jnp.stack([flat_in] * lax.axis_size(("seq", "rep"))), ("seq", "rep"), 0, 0),
+        axis=0,
+    )
     full_out = lax.all_gather(out_panel.T, ("seq", "rep"), axis=0, tiled=True)
     projected = jnp.dot(slab_rows, full_in, preferred_element_type=jnp.float32)
     projected = lax.optimization_barrier(projected)

time: 411 us -> 690 us (1.68)
  waiting for transfers between devices: 296 us -> 559 us
  starting transfers between devices: 0.12 us -> 9.9 us
  local copies, waits for them, and re-layouts: 29.8 us -> 37.6 us
    all_to_all x0 -> x1, waiting for transfers between devices: none -> 335 us  [local(): lax.all_to_all(jnp.stack([flat_in] * lax.axis_size(('seq', 'rep'))), ('se...]
    all_gather x1 -> x0, waiting for transfers between devices: 146 us -> none  [local(): full_in = lax.all_gather(flat_in, ('seq', 'rep'), axis=0, tiled=True)]
    all_gather x1, waiting for transfers between devices: 18.1 us -> 91.8 us  [local(): states = lax.all_gather(local_state.astype(jnp.bfloat16), 'seq')]
    all_to_all x0 -> x1, starting transfers between devices: none -> 9.78 us  [local(): lax.all_to_all(jnp.stack([flat_in] * lax.axis_size(('seq', 'rep'))), ('se...]
    another operation x0 -> x1, local copies, waits for them, and re-layouts: none -> 8.63 us  [local(): jnp.stack([flat_in] * lax.axis_size(('seq', 'rep')))]
    unnamed x8 -> x10, local copies, waits for them, and re-layouts: 19.6 us -> 18.8 us
  transfers between devices with their start and end apart: 4 -> 4, of which waited for: 4 -> 4; matrix products, arithmetic and copies ran while one was open for 8% -> 5% of each run, Pallas kernels for 0% -> 0%
where the time goes in v1:
time: 690 us
  waiting for transfers between devices  559 us (81%)
  matrix products  62.2 us (9%)
  local copies, waits for them, and re-layouts  37.6 us (5%)
  between operations  13.9 us (2%)
  starting transfers between devices  9.9 us (1%)
  other arithmetic  7.48 us (1%)
    all_to_all x1, waiting for transfers between devices, local(): lax.all_to_all(jnp.stack([flat_in] * lax.axis_size(('seq', 'rep'))), ('se...  335 us
    all_gather x1, waiting for transfers between devices, local(): states = lax.all_gather(local_state.astype(jnp.bfloat16), 'seq')  91.8 us
    all_gather x1, waiting for transfers between devices, local(): full_out = lax.all_gather(out_panel.T, ('seq', 'rep'), axis=0, tiled=True)  79.5 us
    reduce_scatter x1, waiting for transfers between devices, local(): lax.psum_scatter(head_partial.astype(jnp.bfloat16), 'tp', scatter_dimensi...  52.2 us
    dot_general x1, matrix products, local(): projected = jnp.dot(slab_rows, full_in, preferred_element_type=jnp.float32)  26 us
    unnamed x10, local copies, waits for them, and re-layouts  18.8 us
  transfers between devices with their start and end apart: 4, of which 4 were waited for; matrix products, arithmetic and copies ran while one was open for 5% of the time, Pallas kernels for 0%

profile of v1, /device:TPU:1, one launch (start us, length us, event | category | flops | bytes accessed | tf_op | source)
XLA Modules:
  0.0 689.9 jit_solution(6597331146889387301)
XLA Ops:
  6.5 1.4 copy.26
  7.9 8.6 %stack.2 = bf16[32,96,4096]{2,1,0:T(8,128)(2,1)} broadcast(bf16[96,4096]{1,0:T(8,128)(2,1)S(1)} %bitcast.68), dimensions={1,2} | broadcast | bytes 25952256 | tf_op jit(solution)/shard_map/stack | solution.py:45
  16.6 9.8 %all-to-all-start = ((bf16[32,96,4096]{2,1,0:T(8,128)(2,1)}), bf16[32,96,4096]{2,1,0:T(8,128)(2,1)}, u32[]{:S(2)}, u32[]{:S(2)}) async-start(bf16[32,96,4096]{2,1,0:T(8,128)(2,1)} %stack.2), calls=%async_computation | async-start | bytes 50331648 | tf_op jit(solution)/shard_map/all_to_all | solution.py:45
  27.2 0.1 exponential_multiply_fusion
  27.2 334.5 %all-to-all-done = bf16[32,96,4096]{2,1,0:T(8,128)(2,1)} async-done(((bf16[32,96,4096]{2,1,0:T(8,128)(2,1)}), bf16[32,96,4096]{2,1,0:T(8,128)(2,1)}, u32[]{:S(2)}, u32[]{:S(2)}) %all-to-all-start) | async-done | bytes 25165856 | tf_op jit(solution)/shard_map/all_to_all | solution.py:45
  361.8 26.0 %fusion.5 = f32[768,4096]{1,0:T(8,128)} fusion(bf16[3072,4096]{1,0:T(8,128)(2,1)} %bitcast.1, bf16[1,768,3072]{2,1,0:T(8,128)(2,1)} %param.5), kind=kOutput, calls=%fused_computation.7 | convolution fusion | flops 19327352832 | bytes 42467328 | tf_op jit(solution)/shard_map/dot_general | solution.py:49
  387.8 12.0 %copy.27 = f32[96,8,32,128]{3,2,1,0:T(8,128)} copy(f32[96,8,32,128]{3,1,2,0:T(8,128)} %bitcast.66) | data formatting | bytes 25165824
  399.8 7.0 %fusion.31 = (f32[768,1,8,128]{3,2,1,0:T(8,128)S(1)}, f32[768,1,8,128]{3,2,1,0:T(8,128)}, f32[768,1,8,128]{3,2,1,0:T(8,128)}) fusion(f32[768,4,8,128]{3,2,1,0:T(8,128)} %bitcast.64), kind=kLoop, calls=%fused_computation.52 | loop fusion | bytes 18874368 | tf_op jit(solution)/shard_map/slice | solution.py:55
  406.8 3.2 slice.17
  410.0 2.9 copy.24
  412.9 4.9 fusion.21
  417.9 0.7 all-gather.4.cloned.1.call-update
  418.7 0.1 exponential_select_fusion
  418.8 1.5 fusion.12
  420.3 1.8 convert_maximum_fusion
  422.0 2.5 copy.25
  424.5 13.6 %fusion = f32[8,128,768]{2,1,0:T(8,128)} fusion(f32[768,768]{1,0:T(8,128)} %convert_maximum_fusion, f32[8]{0:T(128)S(1)} %get-tuple-element.11, pred[768,768]{1,0:T(8,128)(4,1)} %fusion.12, bf16[768,1,8,128]{0,3,2,1:T(8,128)(2,1)} %copy.24, f32[768,1,8,128]{3,2,1,0:T(8,128)} %get-tuple-element.7, f32[768,1,8,128]{3,2,1,0:T(8,128)} %get-tuple-element.6), kind=kOutput, calls=%fused_computation.1 | convolution fusion | flops 2443444224 | bytes 13959200 | tf_op jit(solution)/shard_map/hij,jhd->ihd/dot_general | solution.py:23
  438.1 91.8 %all-gather.6.cloned.1.call-done = bf16[128,128,128]{2,1,0:T(8,128)(2,1)} async-done(((bf16[8,128,128]{2,1,0:T(8,128)(2,1)}), bf16[128,128,128]{2,1,0:T(8,128)(2,1)}) %all-gather.6.cloned.1.call-update) | async-done | bytes 4194320 | tf_op jit(solution)/shard_map/all_gather | solution.py:57
  529.9 3.1 fusion.2
  533.0 8.0 %fusion.8 = (f32[768,8]{0,1:T(8,128)S(1)}, f32[8,128,768]{2,1,0:T(8,128)S(1)}) fusion(f32[8,128,768]{2,1,0:T(8,128)} %fusion, f32[8,128,128]{2,1,0:T(8,128)S(1)} %fusion.2, f32[768,8]{0,1:T(8,128)S(1)} %get-tuple-element.8, f32[768,1,8,128]{3,2,1,0:T(8,128)S(1)} %copy-done.1), kind=kOutput, calls=%fused_computation.15 | convolution fusion | flops 1216604160 | bytes 10010624 | tf_op jit(solution)/shard_map/ihd,hde->ihe/dot_general | solution.py:74
  541.0 0.9 fusion.7
  541.9 79.5 %all-gather.4.cloned.1.call-done = bf16[3072,1024]{1,0:T(8,128)(2,1)} async-done(((bf16[96,1024]{1,0:T(8,128)(2,1)}), bf16[3072,1024]{1,0:T(8,128)(2,1)}) %all-gather.4.cloned.1.call-update) | async-done | bytes 6291472 | tf_op jit(solution)/shard_map/all_gather | solution.py:48
  621.4 9.7 %convolution_convert_fusion = bf16[768,3072]{1,0:T(8,128)(2,1)} fusion(bf16[768,1024]{0,1:T(8,128)(2,1)S(1)} %bitcast.69, bf16[3072,1024]{1,0:T(8,128)(2,1)} %all-gather.4.cloned.1.call-done), kind=kOutput, calls=%fused_computation.6 | convolution fusion | flops 4834197504 | bytes 12582912 | tf_op jit(solution)/shard_map/dot_general | solution.py:83
  631.1 52.2 %reduce-scatter.2.cloned.1.call-done = bf16[768,768]{1,0:T(8,128)(2,1)} async-done(((bf16[768,3072]{1,0:T(8,128)(2,1)}), bf16[768,768]{1,0:T(8,128)(2,1)}) %reduce-scatter.2.cloned.1.call-update) | async-done | bytes 1179664 | tf_op jit(solution)/shard_map/reduce_scatter | solution.py:86
  (19 shorter events, 0.2 us)
Async XLA Ops:
  16.6 10.6 %copy-start.2 = (s32[8]{0:T(128)S(1)}, s32[8]{0:T(128)}, u32[]{:S(2)}) copy-start(s32[8]{0:T(128)} %param.8) | copy-start | bytes 100
  16.6 345.2 %all-to-all-start = ((bf16[32,96,4096]{2,1,0:T(8,128)(2,1)}), bf16[32,96,4096]{2,1,0:T(8,128)(2,1)}, u32[]{:S(2)}, u32[]{:S(2)}) async-start(bf16[32,96,4096]{2,1,0:T(8,128)(2,1)} %stack.2), calls=%async_computation | async-start | bytes 50331648 | tf_op jit(solution)/shard_map/all_to_all | solution.py:45
  26.4 503.5 %all-gather.6.cloned.1.call-start = ((), (), s32[]{:S(2)}) async-start(), calls=%async_computation.4 | async-start | bytes 4456448 | tf_op jit(solution)/shard_map/all_gather | solution.py:57
  417.8 203.6 %all-gather.4.cloned.1.call-start = ((), (), s32[]{:S(2)}) async-start(), calls=%async_computation.2 | async-start | bytes 6488064 | tf_op jit(solution)/shard_map/all_gather | solution.py:48
  418.6 264.8 %reduce-scatter.2.cloned.1.call-start = ((), (), s32[]{:S(2)}) async-start(), calls=%async_computation.3 | async-start | bytes 5898240 | tf_op jit(solution)/shard_map/reduce_scatter | solution.py:86
  438.1 94.9 %copy-start.1 = (f32[768,1,8,128]{3,2,1,0:T(8,128)S(1)}, f32[768,1,8,128]{3,2,1,0:T(8,128)}, u32[]{:S(2)}) copy-start(f32[768,1,8,128]{3,2,1,0:T(8,128)} %get-tuple-element.6) | copy-start | bytes 9437188
  533.0 8.0 %copy-start = (f32[768,1,8,128]{0,3,2,1:T(8,128)S(1)}, f32[768,1,8,128]{0,3,2,1:T(8,128)}, u32[]{:S(2)}) copy-start(f32[768,1,8,128]{0,3,2,1:T(8,128)} %copy.25) | copy-start | bytes 9437188
Sparse Core Ops, SparseCore 0:
  418.0 111.8 all-gather.5
  531.6 89.7 all-gather.3
  631.2 52.0 reduce-scatter.1
